TPU v7x, 32 devices: a whole 2x2x4 slice. The times are simulated.
32 devices in a mesh: grp: 2 (over x), exp: 16 (over z, y, core).
Axes of the slice: x: 2, y: 2, z: 4, core: 2. Of those that a mesh axis runs over, the one named last changes fastest.
Arguments:
- tokens: bfloat16 [128, 6144], P(('grp', 'exp')), parts along dimension 0, may hold values from -6 to 6
- expert_ids: int32 [128, 2], P(('grp', 'exp')), parts along dimension 0, may hold values from 0 to 3, all different within a row; in each aligned block of 4 rows (0 to 3, 4 to 7, ...) at most 3 rows name the same one
- router_weight: bfloat16 [6144, 4], replicated, may hold values from -0.15625 to 0.15625
- gate_weight: bfloat16 [16, 6144, 2048], P('exp'), may hold values from -0.078125 to 0.078125
- up_weight: bfloat16 [16, 6144, 2048], P('exp'), may hold values from -0.078125 to 0.078125
- down_weight: bfloat16 [16, 2048, 6144], P('exp'), may hold values from -0.0625 to 0.0625
Outputs:
- mixed: bfloat16 [128, 6144], P(('grp', 'exp')), parts along dimension 0
There are 2 independent parts, one for each index of `grp`. A program takes and returns all parts, laid end to end along the dimension named above; an argument that names none is the same for every part. Nothing has to cross between parts.
Inputs may be any that keep to these rules, and one draw needn't show every extreme that they name: `expert_ids`: the two ids of a token differ. Among the 4 tokens of one device (rows j * 4 to (j + 1) * 4 - 1), no expert is named more than 3 times, and in every draw some device names some expert exactly 3 times.
All inputs are finite; a program needn't handle non-finite values.
Results may differ from a plain program's by a relative error of at most 0.0059.
Values may be sent and summed in bfloat16 or wider, within the bound.
A program may use at most 192 MiB of HBM per device.

v0:
```python
import jax
import jax.numpy as jnp
from jax import lax
from jax.sharding import PartitionSpec as P

CAP = 3


def swapped(value, axis, distance):
    mask = 2**distance
    pairs = [(source, source ^ mask) for source in range(lax.axis_size(axis))]
    return lax.ppermute(value, axis, pairs)


def from_behind(value, axis, steps):
    count = lax.axis_size(axis)
    pairs = [(source, (source + steps) % count) for source in range(count)]
    return lax.ppermute(value, axis, pairs)


def expert_hidden(row_piece, gate_block, up_block):
    gate_part = jnp.dot(row_piece, gate_block, preferred_element_type=jnp.float32)
    up_part = jnp.dot(row_piece, up_block, preferred_element_type=jnp.float32)
    return (jax.nn.silu(gate_part) * up_part).astype(jnp.bfloat16)


def butterfly(cell_array, my_expert, experts, outward):
    bit_count = experts.bit_length() - 1
    for bit_index in range(bit_count):
        low_span = 1 << bit_index
        high_span = experts // (2 * low_span)
        my_bit = my_expert // low_span % 2
        split_cells = cell_array.reshape((high_span, 2, low_span) + cell_array.shape[1:])
        kept_cells = lax.dynamic_index_in_dim(split_cells, my_bit, 1, keepdims=False)
        sent_cells = lax.dynamic_index_in_dim(split_cells, 1 - my_bit, 1, keepdims=False)
        if outward:
            came_cells = swapped(sent_cells, "exp", bit_index)
        else:
            came_cells = swapped(sent_cells, "exp", bit_index)
        low_first = jnp.stack([kept_cells, came_cells], 1)
        high_first = jnp.stack([came_cells, kept_cells], 1)
        cell_array = jnp.where(my_bit == 0, low_first, high_first).reshape(cell_array.shape)
    return cell_array


def shards(tokens, expert_ids, router_weight, gate_weight, up_weight, down_weight):
    model_width = tokens.shape[1]
    experts = router_weight.shape[1]
    devices = lax.axis_size("exp")
    group_size = devices // experts
    capacity = CAP
    my_index = lax.axis_index("exp")
    my_expert = my_index % experts
    my_slot = my_index // experts
    gate_block = gate_weight[0]
    up_block = up_weight[0]
    down_block = down_weight[0]
    block_rows = experts * capacity
    logits = jnp.dot(tokens, router_weight, preferred_element_type=jnp.float32)
    expert_iota = jnp.arange(experts, dtype=jnp.int32)
    pick_first = expert_ids[:, 0:1] == expert_iota[None, :]
    pick_second = expert_ids[:, 1:2] == expert_iota[None, :]
    logit_first = jnp.sum(jnp.where(pick_first, logits, 0.0), axis=1)
    logit_second = jnp.sum(jnp.where(pick_second, logits, 0.0), axis=1)
    weight_first = 1.0 / (1.0 + jnp.exp(logit_second - logit_first))
    weight_second = 1.0 / (1.0 + jnp.exp(logit_first - logit_second))
    weight_table = jnp.where(pick_first, weight_first[:, None], 0.0) + jnp.where(
        pick_second, weight_second[:, None], 0.0
    )
    routed = (pick_first | pick_second).astype(jnp.int32)
    route_rank = jnp.cumsum(routed, axis=0) - routed
    slot_iota = jnp.arange(capacity, dtype=jnp.int32)
    placement = (routed[:, :, None] == 1) & (route_rank[:, :, None] == slot_iota[None, None, :])
    placement_bf = placement.astype(jnp.bfloat16)
    outgoing = jnp.einsum(
        "tec,td->ecd", placement_bf, tokens, preferred_element_type=jnp.float32
    ).astype(jnp.bfloat16)
    own_rows = butterfly(outgoing, my_expert, experts, True).reshape(block_rows, model_width)
    gathered = lax.dynamic_update_index_in_dim(
        jnp.zeros((group_size, block_rows, model_width), jnp.bfloat16), own_rows, my_slot, 0
    )

    def pass_rows(step_index, loop_state):
        current, gathered_sofar = loop_state
        current = from_behind(current, "exp", experts)
        gathered_sofar = lax.dynamic_update_index_in_dim(
            gathered_sofar, current, (my_slot - step_index - 1) % group_size, 0
        )
        return (current, gathered_sofar)

    current, gathered = lax.fori_loop(0, group_size - 1, pass_rows, (own_rows, gathered))
    all_rows = gathered.reshape(group_size * block_rows, model_width)
    hidden = expert_hidden(all_rows, gate_block, up_block)
    slot_hidden = hidden.reshape(group_size, block_rows, hidden.shape[1])

    def slot_partial(slot_index):
        return jnp.dot(
            lax.dynamic_index_in_dim(slot_hidden, slot_index, 0, keepdims=False),
            down_block,
            preferred_element_type=jnp.float32,
        )

    def add_around(step_index, running):
        running = from_behind(running, "exp", experts)
        return running + slot_partial((my_slot - 2 - step_index) % group_size)

    running = lax.fori_loop(0, group_size - 1, add_around, slot_partial((my_slot - 1) % group_size))
    returned = butterfly(
        running.astype(jnp.bfloat16).reshape(experts, capacity, model_width),
        my_expert,
        experts,
        False,
    )
    selected = jnp.einsum(
        "tec,ecd->ted", placement_bf, returned, preferred_element_type=jnp.float32
    )
    mixed = jnp.sum(weight_table[:, :, None] * selected, axis=1)
    return mixed.astype(jnp.bfloat16)


def solution(mesh):
    return jax.shard_map(
        shards,
        mesh=mesh,
        in_specs=(
            P(("grp", "exp"), None),
            P(("grp", "exp"), None),
            P(),
            P("exp", None, None),
            P("exp", None, None),
            P("exp", None, None),
        ),
        out_specs=P(("grp", "exp"), None),
        check_vma=False,
    )
```

profile of v0, /device:TPU:0, one launch (start us, length us, event | category | flops | bytes accessed | tf_op | source)
XLA Modules:
  0.0 131.2 jit_solution(17403562345458477489)
XLA Ops:
  0.0 0.8 slice_bitcast_fusion.1
  1.5 0.3 constant_dynamic-slice_fusion.7
  1.9 0.5 collective-permute-start.2
  2.5 0.8 collective-permute-done.2
  3.3 0.2 broadcast_select_fusion.1
  3.5 0.3 constant_dynamic-slice_fusion.5
  3.9 2.9 %collective-permute-start.3 = (bf16[1,2,3,6144]{3,1,2,0:T(2,128)(2,1)S(1)}, bf16[1,2,3,6144]{3,1,2,0:T(2,128)(2,1)S(1)}, u32[]{:S(2)}, u32[]{:S(2)}) collective-permute-start(bf16[1,2,3,6144]{3,1,2,0:T(2,128)(2,1)S(1)} %bitcast.79), channel_id=1, source_target_pairs={{0,2},{1,3},{2,0},{3,1},{4,6},{5,7},{6,4},{7,5},{8,10},{9,11},{10,... | collective-permute-start | bytes 221192 | tf_op jit(solution)/shard_map/ppermute | solution.py:12
  6.9 1.0 select_reduce_fusion.1
  7.9 1.5 %collective-permute-done.3 = bf16[1,2,3,6144]{3,1,2,0:T(2,128)(2,1)S(1)} collective-permute-done((bf16[1,2,3,6144]{3,1,2,0:T(2,128)(2,1)S(1)}, bf16[1,2,3,6144]{3,1,2,0:T(2,128)(2,1)S(1)}, u32[]{:S(2)}, u32[]{:S(2)}) %collective-permute-start.3) | collective-permute-done | bytes 73760 | tf_op jit(solution)/shard_map/ppermute | solution.py:12
  9.5 0.2 broadcast_select_fusion.3
  10.1 23.5 %while.32 = (s32[]{:T(128)}, bf16[12,6144]{1,0:T(8,128)(2,1)S(1)}, bf16[4,12,6144]{2,1,0:T(8,128)(2,1)S(1)}, s32[]{:T(128)}, s32[]{:T(128)}, /*index=5*/s32[]{:T(128)}, s32[]{:T(128)}, s32[]{:T(128)}, s32[]{:T(128)}) while((s32[]{:T(128)}, bf16[12,6144]{1,0:T(8,128)(2,1)S(1)}, bf16[4,12,6144]{2,1,0:T(8,128)(2,1)S(1)}, s32[]{:T(128)}, ...), condition=%wide.region_4.5_spmd, body=%wide.region_3.4_spmd.sunk | while | flops 18 | bytes 1278256 | solution.py:91
  10.2 1.9 %collective-permute-start = (bf16[12,6144]{1,0:T(8,128)(2,1)S(1)}, bf16[12,6144]{1,0:T(8,128)(2,1)S(1)}, u32[]{:S(2)}, u32[]{:S(2)}) collective-permute-start(bf16[12,6144]{1,0:T(8,128)(2,1)S(1)} %get-tuple-element.355), channel_id=1, source_target_pairs={{0,4},{1,5},{2,6},{3,7},{4,8},{5,9},{6,10},{7,11},{8,12},{9,13},{1... | collective-permute-start | bytes 442376 | tf_op jit(solution)/shard_map/while/body/eval_jaxpr/ppermute | solution.py:18
  12.0 6.4 %collective-permute-done = bf16[12,6144]{1,0:T(8,128)(2,1)S(1)} collective-permute-done((bf16[12,6144]{1,0:T(8,128)(2,1)S(1)}, bf16[12,6144]{1,0:T(8,128)(2,1)S(1)}, u32[]{:S(2)}, u32[]{:S(2)}) %collective-permute-start) | collective-permute-done | bytes 147488 | tf_op jit(solution)/shard_map/while/body/eval_jaxpr/ppermute | solution.py:18
  18.6 7.4 %collective-permute-done = bf16[12,6144]{1,0:T(8,128)(2,1)S(1)} collective-permute-done((bf16[12,6144]{1,0:T(8,128)(2,1)S(1)}, bf16[12,6144]{1,0:T(8,128)(2,1)S(1)}, u32[]{:S(2)}, u32[]{:S(2)}) %collective-permute-start) | collective-permute-done | bytes 147488 | tf_op jit(solution)/shard_map/while/body/eval_jaxpr/ppermute | solution.py:18
  26.2 7.4 %collective-permute-done = bf16[12,6144]{1,0:T(8,128)(2,1)S(1)} collective-permute-done((bf16[12,6144]{1,0:T(8,128)(2,1)S(1)}, bf16[12,6144]{1,0:T(8,128)(2,1)S(1)}, u32[]{:S(2)}, u32[]{:S(2)}) %collective-permute-start) | collective-permute-done | bytes 147488 | tf_op jit(solution)/shard_map/while/body/eval_jaxpr/ppermute | solution.py:18
  33.8 10.5 %fusion.5 = f32[48,2048]{1,0:T(8,128)S(1)} fusion(bf16[48,6144]{1,0:T(8,128)(2,1)S(1)} %reshape.420, bf16[1,6144,2048]{2,1,0:T(8,128)(2,1)} %param.13), kind=kOutput, calls=%fused_computation.7 | convolution fusion | flops 1207959552 | bytes 26148864 | tf_op jit(solution)/shard_map/dot_general | solution.py:22
  44.3 10.6 %fusion.11 = bf16[48,2048]{1,0:T(8,128)(2,1)S(1)} fusion(bf16[48,6144]{1,0:T(8,128)(2,1)S(1)} %reshape.420, bf16[1,6144,2048]{2,1,0:T(8,128)(2,1)} %param.14, f32[48,2048]{1,0:T(8,128)S(1)} %fusion.5), kind=kOutput, calls=%fused_computation.13 | convolution fusion | flops 1208549376 | bytes 26345472 | tf_op jit(solution)/shard_map/dot_general | solution.py:23
  54.9 9.9 %fusion.15 = f32[12,6144]{1,0:T(8,128)S(1)} fusion(bf16[4,12,2048]{2,1,0:T(8,128)(2,1)S(1)} %reshape.421, s32[]{:T(128)S(6)} %select_n.218, bf16[1,2048,6144]{2,1,0:T(8,128)(2,1)} %param.15), kind=kOutput, calls=%fused_computation.25 | convolution fusion | flops 301989888 | bytes 25526276 | tf_op jit(solution)/shard_map/dot_general | solution.py:97
  64.9 58.4 %while.33 = (s32[]{:T(128)}, f32[12,6144]{1,0:T(8,128)S(1)}, s32[]{:T(128)}, bf16[4,12,2048]{2,1,0:T(8,128)(2,1)S(1)}, bf16[2048,6144]{1,0:T(8,128)(2,1)}, /*index=5*/s32[]{:T(128)}, s32[]{:T(128)}, s32[]{:T(128)}, s32[]{:T(128)}) while((s32[]{:T(128)}, f32[12,6144]{1,0:T(8,128)S(1)}, s32[]{:T(128)}, bf16[4,12,2048]{2,1,0:T(8,128)(2,1)S(1)}, ...), condition=%wide.region_6.7_spmd, body=%wide.region_5.6_spmd.sunk | while | flops 302063616 | bytes 27099428 | solution.py:107
  64.9 9.6 %collective-permute-done.1 = f32[12,6144]{1,0:T(8,128)S(1)} collective-permute-done((f32[12,6144]{1,0:T(8,128)S(1)}, f32[12,6144]{1,0:T(8,128)S(1)}, u32[]{:S(2)}, u32[]{:S(2)}) %collective-permute-start.1) | collective-permute-done | bytes 294944 | tf_op jit(solution)/shard_map/while/body/eval_jaxpr/ppermute | solution.py:18
  74.4 9.9 %convolution_add_fusion.2 = f32[12,6144]{1,0:T(8,128)S(1)} fusion(f32[12,6144]{1,0:T(8,128)S(1)} %collective-permute-done.1, bf16[2048,6144]{1,0:T(8,128)(2,1)} %get-tuple-element.394, bf16[4,12,2048]{2,1,0:T(8,128)(2,1)S(1)} %get-tuple-element.393, s32[]{:T(128)S(6)} %select_n.241), kind=kOutput, calls=%fused_computation.1.clone.1 | convolution fusion | flops 302063616 | bytes 25919492 | tf_op jit(solution)/shard_map/while/body/eval_jaxpr/dot_general | solution.py:97
  84.4 9.6 %collective-permute-done.1 = f32[12,6144]{1,0:T(8,128)S(1)} collective-permute-done((f32[12,6144]{1,0:T(8,128)S(1)}, f32[12,6144]{1,0:T(8,128)S(1)}, u32[]{:S(2)}, u32[]{:S(2)}) %collective-permute-start.1) | collective-permute-done | bytes 294944 | tf_op jit(solution)/shard_map/while/body/eval_jaxpr/ppermute | solution.py:18
  93.9 9.9 %convolution_add_fusion.2 = f32[12,6144]{1,0:T(8,128)S(1)} fusion(f32[12,6144]{1,0:T(8,128)S(1)} %collective-permute-done.1, bf16[2048,6144]{1,0:T(8,128)(2,1)} %get-tuple-element.394, bf16[4,12,2048]{2,1,0:T(8,128)(2,1)S(1)} %get-tuple-element.393, s32[]{:T(128)S(6)} %select_n.241), kind=kOutput, calls=%fused_computation.1.clone.1 | convolution fusion | flops 302063616 | bytes 25919492 | tf_op jit(solution)/shard_map/while/body/eval_jaxpr/dot_general | solution.py:97
  103.8 9.6 %collective-permute-done.1 = f32[12,6144]{1,0:T(8,128)S(1)} collective-permute-done((f32[12,6144]{1,0:T(8,128)S(1)}, f32[12,6144]{1,0:T(8,128)S(1)}, u32[]{:S(2)}, u32[]{:S(2)}) %collective-permute-start.1) | collective-permute-done | bytes 294944 | tf_op jit(solution)/shard_map/while/body/eval_jaxpr/ppermute | solution.py:18
  113.4 9.9 %convolution_add_fusion.2 = f32[12,6144]{1,0:T(8,128)S(1)} fusion(f32[12,6144]{1,0:T(8,128)S(1)} %collective-permute-done.1, bf16[2048,6144]{1,0:T(8,128)(2,1)} %get-tuple-element.394, bf16[4,12,2048]{2,1,0:T(8,128)(2,1)S(1)} %get-tuple-element.393, s32[]{:T(128)S(6)} %select_n.241), kind=kOutput, calls=%fused_computation.1.clone.1 | convolution fusion | flops 302063616 | bytes 25919492 | tf_op jit(solution)/shard_map/while/body/eval_jaxpr/dot_general | solution.py:97
  123.8 1.1 collective-permute-done.4
  124.9 0.2 broadcast_select_fusion
  125.2 0.3 constant_dynamic-slice_fusion.1
  125.6 1.3 collective-permute-start.5
  126.9 3.1 %collective-permute-done.5 = bf16[1,2,3,6144]{3,1,2,0:T(2,128)(2,1)S(1)} collective-permute-done((bf16[1,2,3,6144]{3,1,2,0:T(2,128)(2,1)S(1)}, bf16[1,2,3,6144]{3,1,2,0:T(2,128)(2,1)S(1)}, u32[]{:S(2)}, u32[]{:S(2)}) %collective-permute-start.5) | collective-permute-done | bytes 73760 | tf_op jit(solution)/shard_map/ppermute | solution.py:12
  130.0 0.2 broadcast_select_fusion.2
  130.3 0.9 fusion.14
  (44 shorter events, 2.6 us)
Async XLA Ops:
  0.0 1.2 copy-start
  1.9 1.4 %collective-permute-start.2 = (bf16[2,1,3,6144]{3,0,2,1:T(2,128)(2,1)S(1)}, bf16[2,1,3,6144]{3,0,2,1:T(2,128)(2,1)S(1)}, u32[]{:S(2)}, u32[]{:S(2)}) collective-permute-start(bf16[2,1,3,6144]{3,0,2,1:T(2,128)(2,1)S(1)} %bitcast.77), channel_id=1, source_target_pairs={{0,1},{1,0},{2,3},{3,2},{4,5},{5,4},{6,7},{7,6},{8,9},{9,8},{10,11... | collective-permute-start | bytes 221192 | tf_op jit(solution)/shard_map/ppermute | solution.py:12
  3.9 5.5 %collective-permute-start.3 = (bf16[1,2,3,6144]{3,1,2,0:T(2,128)(2,1)S(1)}, bf16[1,2,3,6144]{3,1,2,0:T(2,128)(2,1)S(1)}, u32[]{:S(2)}, u32[]{:S(2)}) collective-permute-start(bf16[1,2,3,6144]{3,1,2,0:T(2,128)(2,1)S(1)} %bitcast.79), channel_id=1, source_target_pairs={{0,2},{1,3},{2,0},{3,1},{4,6},{5,7},{6,4},{7,5},{8,10},{9,11},{10,... | collective-permute-start | bytes 221192 | tf_op jit(solution)/shard_map/ppermute | solution.py:12
  10.2 8.3 %collective-permute-start = (bf16[12,6144]{1,0:T(8,128)(2,1)S(1)}, bf16[12,6144]{1,0:T(8,128)(2,1)S(1)}, u32[]{:S(2)}, u32[]{:S(2)}) collective-permute-start(bf16[12,6144]{1,0:T(8,128)(2,1)S(1)} %get-tuple-element.355), channel_id=1, source_target_pairs={{0,4},{1,5},{2,6},{3,7},{4,8},{5,9},{6,10},{7,11},{8,12},{9,13},{1... | collective-permute-start | bytes 442376 | tf_op jit(solution)/shard_map/while/body/eval_jaxpr/ppermute | solution.py:18
  18.5 7.5 %collective-permute-start = (bf16[12,6144]{1,0:T(8,128)(2,1)S(1)}, bf16[12,6144]{1,0:T(8,128)(2,1)S(1)}, u32[]{:S(2)}, u32[]{:S(2)}) collective-permute-start(bf16[12,6144]{1,0:T(8,128)(2,1)S(1)} %get-tuple-element.355), channel_id=1, source_target_pairs={{0,4},{1,5},{2,6},{3,7},{4,8},{5,9},{6,10},{7,11},{8,12},{9,13},{1... | collective-permute-start | bytes 442376 | tf_op jit(solution)/shard_map/while/body/eval_jaxpr/ppermute | solution.py:18
  26.1 7.5 %collective-permute-start = (bf16[12,6144]{1,0:T(8,128)(2,1)S(1)}, bf16[12,6144]{1,0:T(8,128)(2,1)S(1)}, u32[]{:S(2)}, u32[]{:S(2)}) collective-permute-start(bf16[12,6144]{1,0:T(8,128)(2,1)S(1)} %get-tuple-element.355), channel_id=1, source_target_pairs={{0,4},{1,5},{2,6},{3,7},{4,8},{5,9},{6,10},{7,11},{8,12},{9,13},{1... | collective-permute-start | bytes 442376 | tf_op jit(solution)/shard_map/while/body/eval_jaxpr/ppermute | solution.py:18
  64.9 9.6 %collective-permute-start.1 = (f32[12,6144]{1,0:T(8,128)S(1)}, f32[12,6144]{1,0:T(8,128)S(1)}, u32[]{:S(2)}, u32[]{:S(2)}) collective-permute-start(f32[12,6144]{1,0:T(8,128)S(1)} %get-tuple-element.382), channel_id=1, source_target_pairs={{0,4},{1,5},{2,6},{3,7},{4,8},{5,9},{6,10},{7,11},{8,12},{9,13},{1... | collective-permute-start | bytes 884744 | tf_op jit(solution)/shard_map/while/body/eval_jaxpr/ppermute | solution.py:18
  84.3 9.6 %collective-permute-start.1 = (f32[12,6144]{1,0:T(8,128)S(1)}, f32[12,6144]{1,0:T(8,128)S(1)}, u32[]{:S(2)}, u32[]{:S(2)}) collective-permute-start(f32[12,6144]{1,0:T(8,128)S(1)} %get-tuple-element.382), channel_id=1, source_target_pairs={{0,4},{1,5},{2,6},{3,7},{4,8},{5,9},{6,10},{7,11},{8,12},{9,13},{1... | collective-permute-start | bytes 884744 | tf_op jit(solution)/shard_map/while/body/eval_jaxpr/ppermute | solution.py:18
  103.8 9.6 %collective-permute-start.1 = (f32[12,6144]{1,0:T(8,128)S(1)}, f32[12,6144]{1,0:T(8,128)S(1)}, u32[]{:S(2)}, u32[]{:S(2)}) collective-permute-start(f32[12,6144]{1,0:T(8,128)S(1)} %get-tuple-element.382), channel_id=1, source_target_pairs={{0,4},{1,5},{2,6},{3,7},{4,8},{5,9},{6,10},{7,11},{8,12},{9,13},{1... | collective-permute-start | bytes 884744 | tf_op jit(solution)/shard_map/while/body/eval_jaxpr/ppermute | solution.py:18
  123.3 7.9 %copy-start.1 = (bf16[4,6144]{1,0:T(4,128)(2,1)S(1)}, bf16[4,6144]{1,0:T(4,128)(2,1)}, u32[]{:S(2)}) copy-start(bf16[4,6144]{1,0:T(4,128)(2,1)} %param.10) | copy-start | bytes 147460
  123.6 1.3 %collective-permute-start.4 = (bf16[2,1,3,6144]{3,0,2,1:T(2,128)(2,1)S(1)}, bf16[2,1,3,6144]{3,0,2,1:T(2,128)(2,1)S(1)}, u32[]{:S(2)}, u32[]{:S(2)}) collective-permute-start(bf16[2,1,3,6144]{3,0,2,1:T(2,128)(2,1)S(1)} %bitcast.83), channel_id=1, source_target_pairs={{0,1},{1,0},{2,3},{3,2},{4,5},{5,4},{6,7},{7,6},{8,9},{9,8},{10,11... | collective-permute-start | bytes 221192 | tf_op jit(solution)/shard_map/ppermute | solution.py:12
  125.6 4.4 %collective-permute-start.5 = (bf16[1,2,3,6144]{3,1,2,0:T(2,128)(2,1)S(1)}, bf16[1,2,3,6144]{3,1,2,0:T(2,128)(2,1)S(1)}, u32[]{:S(2)}, u32[]{:S(2)}) collective-permute-start(bf16[1,2,3,6144]{3,1,2,0:T(2,128)(2,1)S(1)} %bitcast.78), channel_id=1, source_target_pairs={{0,2},{1,3},{2,0},{3,1},{4,6},{5,7},{6,4},{7,5},{8,10},{9,11},{10,... | collective-permute-start | bytes 221192 | tf_op jit(solution)/shard_map/ppermute | solution.py:12
where the time goes:
time: 131 us
  matrix products  62.7 us (48%)
  waiting for transfers between devices  56.5 us (43%)
  starting transfers between devices  6.78 us (5%)
  local copies, waits for them, and re-layouts  3.59 us (3%)
    ppermute x6, waiting for transfers between devices, from_behind(): return lax.ppermute(value, axis, pairs)  50 us
    dot_general x4, matrix products, slot_partial(): jnp.dot(lax.dynamic_index_in_dim(slot_hidden, slot_index, 0, keepdims=Fal...  39.6 us
    dot_general x1, matrix products, expert_hidden(): up_part = jnp.dot(row_piece, up_block, preferred_element_type=jnp.float32)  10.6 us
    dot_general x1, matrix products, expert_hidden(): jnp.dot(row_piece, gate_block, preferred_element_type=jnp.float32)  10.5 us
    ppermute x4, waiting for transfers between devices, swapped(): return lax.ppermute(value, axis, pairs)  6.55 us
    ppermute x4, starting transfers between devices, swapped(): return lax.ppermute(value, axis, pairs)  4.78 us
  transfers between devices with their start and end apart: 10, of which 10 were waited for; matrix products, arithmetic and copies ran while one was open for 1% of the time, Pallas kernels for 0%

commit v1 on v0

v1 whole, which is shorter than its diff:
```python
import functools

import jax
import jax.numpy as jnp
from jax import lax
from jax.experimental import pallas as pl
from jax.experimental.pallas import tpu as pltpu
from jax.sharding import PartitionSpec as P

MESH = pl.DeviceIdType.MESH
F32 = jnp.float32
BF16 = jnp.bfloat16
LANES = 128
PLANE = 4
ROWS = 16


def divisor_at_most(total, most):
    return max(size for size in range(LANES, most + 1, LANES) if total % size == 0)


class Plan:
    def __init__(self, devices, tok, width, hidden):
        self.devices, self.tok, self.width, self.hidden = devices, tok, width, hidden
        self.slots = devices // PLANE
        self.pieces = ROWS // tok
        self.piece = width // self.pieces
        self.ext = self.piece + LANES
        self.tokens = devices * tok
        self.half = self.tokens // 2
        self.quarter = self.tokens // 4
        self.up_rows = divisor_at_most(width, min(2048, 2 * hidden))
        self.up_cols = divisor_at_most(hidden, 512)
        self.k_steps = width // self.up_rows
        self.n_steps = hidden // self.up_cols
        self.per_n = 2 * self.k_steps
        self.first = self.per_n * self.n_steps
        self.down_cols = divisor_at_most(width, 512)
        self.downs = width // self.down_cols
        self.buffers = max(self.first, self.downs)
        self.group = 2
        self.groups = self.downs // self.group
        self.cols = self.group * self.down_cols
        self.part = self.cols // self.pieces


def kernel(
    p, experts, tok_ref, ids_ref, router_ref, gate_ref, up_ref, down_ref, out_ref,
    wbuf, x, stage, lhs, hid, table, keep, a_send, a_recv, b_own, b_send, b_recv,
    z_full, z_stage, z_send, z_recv, out_f32,
    wsem, gs_z, gr_z, gs_y, gr_y, gs_c, gr_c, sa, ra, sb, rb, sc, rc,
):
    grp = lax.axis_index("grp")
    me = lax.axis_index("exp")
    slot, e = me // PLANE, me % PLANE
    core, ypos = e % 2, e // 2
    core_peer = slot * PLANE + ypos * 2 + (1 - core)
    y_peer = slot * PLANE + (1 - ypos) * 2 + core

    def first_copy(n, m):
        k, ref = m // 2, (gate_ref, up_ref)[m % 2]
        at = n * p.per_n + m
        cols = pl.ds(pl.multiple_of(n * p.up_cols, p.up_cols), p.up_cols)
        return pltpu.make_async_copy(
            ref.at[0, pl.ds(k * p.up_rows, p.up_rows), cols],
            wbuf.at[at, pl.ds(0, p.up_rows), pl.ds(0, p.up_cols)],
            wsem.at[at],
        )

    def down_copy(j):
        cols = pl.ds(pl.multiple_of(j * p.down_cols, p.down_cols), p.down_cols)
        return pltpu.make_async_copy(
            down_ref.at[0, :, cols],
            wbuf.at[j, pl.ds(0, p.hidden), pl.ds(0, p.down_cols)],
            wsem.at[j],
        )

    def remote(src, dst, send, recv, device):
        return pltpu.make_async_remote_copy(
            src_ref=src, dst_ref=dst, send_sem=send, recv_sem=recv,
            device_id=(grp, device), device_id_type=MESH,
        )

    barrier = pltpu.get_barrier_semaphore()
    z_peers = [lax.rem(slot + d, p.slots) * PLANE + e for d in range(1, p.slots)]
    for peer in z_peers + [y_peer, core_peer]:
        pl.semaphore_signal(barrier, inc=1, device_id=(grp, peer), device_id_type=MESH)

    for m in range(p.per_n):
        first_copy(0, m).start()

    lane = lax.broadcasted_iota(jnp.int32, (p.tok, LANES), 1)
    line = lax.broadcasted_iota(jnp.int32, (p.tok, LANES), 0)
    ids = jnp.zeros((p.tok, LANES), jnp.int32)
    for t in range(p.tok):
        named = jnp.where(lane < LANES // 2, ids_ref[0, t], ids_ref[1, t])
        ids = jnp.where(line == t, named, ids)
    for c in range(p.pieces):
        rows = pl.ds(c * p.tok, p.tok)
        stage[rows, pl.ds(0, p.piece)] = tok_ref[:, pl.ds(c * p.piece, p.piece)].astype(F32)
        stage[rows, pl.ds(p.piece, LANES)] = ids.astype(F32)
    x[me] = stage[...].astype(BF16)

    pl.semaphore_wait(barrier, p.slots + 1)

    started = []

    def send(copy):
        copy.start()
        started.append(copy)

    for d in range(1, p.slots):
        send(remote(x.at[me], x.at[me], gs_z.at[d], gr_z.at[d], z_peers[d - 1]))
    send(remote(x.at[me], x.at[me], gs_y.at[0], gr_y.at[0], y_peer))
    send(remote(x.at[me], x.at[me], gs_c.at[0], gr_c.at[0], core_peer))

    for n in range(1, p.n_steps):
        for m in range(p.per_n):
            first_copy(n, m).start()
    for j in range(p.first, p.downs):
        down_copy(j).start()

    for d in range(1, p.slots):
        block = lax.rem(slot + p.slots - d, p.slots) * PLANE + e
        remote(x.at[block], x.at[block], gs_z.at[d], gr_z.at[d], me ^ 1).wait_recv()
        send(remote(x.at[block], x.at[block], gs_y.at[d], gr_y.at[d], y_peer))
        send(remote(x.at[block], x.at[block], gs_c.at[d], gr_c.at[d], core_peer))
    for d in range(p.slots):
        block = lax.rem(slot + p.slots - d, p.slots) * PLANE + (1 - ypos) * 2 + core
        remote(x.at[block], x.at[block], gs_y.at[d], gr_y.at[d], y_peer).wait_recv()
        at = p.slots + d
        send(remote(x.at[block], x.at[block], gs_c.at[at], gr_c.at[at], core_peer))
    for d in range(p.slots):
        for side in range(2):
            ye = ypos if side == 0 else 1 - ypos
            block = lax.rem(slot + p.slots - d, p.slots) * PLANE + ye * 2 + (1 - core)
            at = side * p.slots + d
            remote(x.at[block], x.at[block], gs_c.at[at], gr_c.at[at], core_peer).wait_recv()

    blocks = p.quarter
    row_in = lax.broadcasted_iota(jnp.int32, (p.quarter, p.devices * ROWS), 0)
    col_in = lax.broadcasted_iota(jnp.int32, (p.quarter, p.devices * ROWS), 1)
    for q in range(PLANE):
        dest_core, dest_y = q // 2, q % 2
        device = (row_in // p.tok) * PLANE + dest_y * 2 + dest_core
        for c in range(p.pieces):
            pick = (col_in == device * ROWS + c * p.tok + row_in % p.tok)
            pick = jnp.where(pick, 1.0, 0.0).astype(BF16)
            flat = x[...].reshape(p.devices * ROWS, p.ext)
            got = jnp.dot(pick, flat, preferred_element_type=F32)
            lhs[pl.ds(q * p.quarter, p.quarter), pl.ds(c * p.piece, p.piece)] = (
                got[:, : p.piece].astype(BF16)
            )
            if c == 0:
                table[pl.ds(q * p.quarter, p.quarter), :] = got[:, p.piece:]

    @pl.loop(0, p.n_steps)
    def _(n):
        sums = [None, None]
        for m in range(p.per_n):
            first_copy(n, m).wait()
            k = m // 2
            part = jnp.dot(
                lhs[:, pl.ds(k * p.up_rows, p.up_rows)],
                wbuf[n * p.per_n + m, pl.ds(0, p.up_rows), pl.ds(0, p.up_cols)],
                preferred_element_type=F32,
            )
            sums[m % 2] = part if k == 0 else sums[m % 2] + part
        g, u = sums
        cols = pl.ds(pl.multiple_of(n * p.up_cols, p.up_cols), p.up_cols)
        hid[:, cols] = (g / (1.0 + jnp.exp(-g)) * u).astype(BF16)
        for m in range(p.per_n):
            @pl.when(n * p.per_n + m < p.downs)
            def _():
                down_copy(n * p.per_n + m).start()

    logits = lax.dot_general(
        lhs[...], router_ref[...], (((1,), (1,)), ((), ())), preferred_element_type=F32
    )
    ids = table[...]
    id_a, id_b = ids[:, 0:1], ids[:, LANES // 2 : LANES // 2 + 1]
    iota = lax.broadcasted_iota(jnp.int32, logits.shape, 1).astype(F32)
    logit_a = jnp.sum(jnp.where(iota == id_a, logits, 0.0), axis=1, keepdims=True)
    logit_b = jnp.sum(jnp.where(iota == id_b, logits, 0.0), axis=1, keepdims=True)
    mine = e.astype(F32)
    weight = jnp.where(id_a == mine, 1.0 / (1.0 + jnp.exp(logit_b - logit_a)), 0.0)
    weight += jnp.where(id_b == mine, 1.0 / (1.0 + jnp.exp(logit_a - logit_b)), 0.0)
    table[...] = jnp.broadcast_to(weight, table.shape)

    def copy_a(g):
        return remote(a_send.at[g], a_recv.at[g], sa.at[g], ra.at[g], core_peer)

    def copy_b(g):
        return remote(b_send.at[g], b_recv.at[g], sb.at[g], rb.at[g], y_peer)

    def copy_c(g, d):
        dest = lax.rem(slot + d, p.slots)
        return remote(
            z_send.at[g, dest], z_recv.at[g, d], sc.at[g, d], rc.at[g, d],
            dest * PLANE + e,
        )

    def compute(g):
        for i in range(p.group):
            j = g * p.group + i
            down_copy(j).wait()
            part = jnp.dot(
                hid[...], wbuf[j, pl.ds(0, p.hidden), pl.ds(0, p.down_cols)],
                preferred_element_type=F32,
            )
            part = part * table[:, 0:1]
            cols = pl.ds(i * p.down_cols, p.down_cols)
            low, high = part[: p.half], part[p.half :]
            is_low = core == 0
            keep[g, :, cols] = jnp.where(is_low, low, high)
            a_send[g, :, cols] = jnp.where(is_low, high, low).astype(BF16)
        copy_a(g).start()

    def second(g):
        copy_a(g).wait()
        total = keep[g] + a_recv[g].astype(F32)
        low, high = total[: p.quarter], total[p.quarter :]
        b_own[g] = jnp.where(ypos == 0, low, high)
        b_send[g] = jnp.where(ypos == 0, high, low).astype(BF16)
        copy_b(g).start()

    def third(g):
        copy_b(g).wait()
        z_full[...] = b_own[g] + b_recv[g].astype(F32)
        for s in range(p.slots):
            for c in range(p.pieces):
                z_stage[s, pl.ds(c * p.tok, p.tok), :] = z_full[
                    pl.ds(s * p.tok, p.tok), pl.ds(c * p.part, p.part)
                ]
        z_send[g] = z_stage[...].astype(BF16)
        b_own[g, pl.ds(0, ROWS), pl.ds(0, p.part)] = z_stage[slot]
        for d in range(1, p.slots):
            copy_c(g, d).start()

    @pl.loop(0, p.groups + 2)
    def _(it):
        @pl.when(it < p.groups)
        def _():
            compute(it)

        @pl.when((it >= 1) & (it < p.groups + 1))
        def _():
            second(it - 1)

        @pl.when(it >= 2)
        def _():
            third(it - 2)

    @pl.loop(0, p.groups)
    def _(g):
        total = b_own[g, pl.ds(0, ROWS), pl.ds(0, p.part)]
        for d in range(1, p.slots):
            copy_c(g, d).wait()
            total = total + z_recv[g, d].astype(F32)
        out_f32[...] = total
        for c in range(p.pieces):
            at = pl.multiple_of(g * p.cols + c * p.part, p.part)
            out_ref[:, pl.ds(at, p.part)] = out_f32[pl.ds(c * p.tok, p.tok), :].astype(BF16)

    for copy in started:
        copy.wait_send()


def shards(devices, tokens, expert_ids, router_weight, gate_weight, up_weight, down_weight):
    tok, width = tokens.shape
    experts = router_weight.shape[1]
    hidden = gate_weight.shape[2]
    p = Plan(devices, tok, width, hidden)
    vmem = pl.BlockSpec(memory_space=pltpu.VMEM)
    hbm = pl.BlockSpec(memory_space=pl.ANY)
    dma = pltpu.SemaphoreType.DMA
    scratch = [
        pltpu.VMEM((p.buffers, max(p.up_rows, hidden), max(p.up_cols, p.down_cols)), BF16),
        pltpu.VMEM((devices, ROWS, p.ext), BF16),
        pltpu.VMEM((ROWS, p.ext), F32),
        pltpu.VMEM((p.tokens, width), BF16),
        pltpu.VMEM((p.tokens, hidden), BF16),
        pltpu.VMEM((p.tokens, LANES), F32),
        pltpu.VMEM((p.groups, p.half, p.cols), F32),
        pltpu.VMEM((p.groups, p.half, p.cols), BF16),
        pltpu.VMEM((p.groups, p.half, p.cols), BF16),
        pltpu.VMEM((p.groups, p.quarter, p.cols), F32),
        pltpu.VMEM((p.groups, p.quarter, p.cols), BF16),
        pltpu.VMEM((p.groups, p.quarter, p.cols), BF16),
        pltpu.VMEM((p.quarter, p.cols), F32),
        pltpu.VMEM((p.slots, ROWS, p.part), F32),
        pltpu.VMEM((p.groups, p.slots, ROWS, p.part), BF16),
        pltpu.VMEM((p.groups, p.slots, ROWS, p.part), BF16),
        pltpu.VMEM((ROWS, p.part), F32),
        dma((p.buffers,)),
        dma((p.slots,)), dma((p.slots,)), dma((p.slots,)), dma((p.slots,)),
        dma((2 * p.slots,)), dma((2 * p.slots,)),
        dma((p.groups,)), dma((p.groups,)), dma((p.groups,)), dma((p.groups,)),
        dma((p.groups, p.slots)), dma((p.groups, p.slots)),
    ]
    return pl.pallas_call(
        functools.partial(kernel, p, experts),
        out_shape=jax.ShapeDtypeStruct((tok, width), BF16),
        in_specs=[vmem, pl.BlockSpec(memory_space=pltpu.SMEM), vmem, hbm, hbm, hbm],
        out_specs=vmem,
        scratch_shapes=scratch,
        compiler_params=pltpu.CompilerParams(
            collective_id=0, has_side_effects=True, vmem_limit_bytes=60 * 2**20
        ),
        cost_estimate=pl.CostEstimate(
            flops=6 * p.tokens * width * hidden,
            bytes_accessed=6 * width * hidden,
            transcendentals=p.tokens * hidden,
        ),
        name="moe_decode",
    )(tokens, expert_ids.T, router_weight.T, gate_weight, up_weight, down_weight)


def solution(mesh):
    return jax.shard_map(
        functools.partial(shards, mesh.shape["exp"]),
        mesh=mesh,
        in_specs=(
            P(("grp", "exp"), None),
            P(("grp", "exp"), None),
            P(),
            P("exp", None, None),
            P("exp", None, None),
            P("exp", None, None),
        ),
        out_specs=P(("grp", "exp"), None),
        check_vma=False,
    )
```

time: 131 us -> 50.5 us (0.39)
  matrix products: 62.7 us -> 0 us
  waiting for transfers between devices: 56.5 us -> 0 us
  Pallas kernels: 0 us -> 48.9 us
  starting transfers between devices: 6.78 us -> 0 us
  local copies, waits for them, and re-layouts: 3.59 us -> 1.44 us
    dot_general x9 -> x0, matrix products: 62.7 us -> none  [the longest x4 39.6 us: slot_partial(): jnp.dot(lax.dynamic_index_in_dim(slot_hidden, slot_index, 0, keepdims=Fal...]
    ppermute x10 -> x0, waiting for transfers between devices: 56.5 us -> none  [the longest x6 50 us: from_behind(): return lax.ppermute(value, axis, pairs)]
    pallas_call x0 -> x1, Pallas kernels: none -> 48.9 us  [shards(): pl.pallas_call(functools.partial(kernel, p, experts), out_shape=jax.Shape...]
    ppermute x10 -> x0, starting transfers between devices: 6.78 us -> none  [the longest x4 4.78 us: swapped(): return lax.ppermute(value, axis, pairs)]
    dynamic_slice x9 -> x0, local copies, waits for them, and re-layouts: 1.42 us -> none  [the longest x6 1.18 us: butterfly(): lax.dynamic_index_in_dim(split_cells, my_bit, 1, keepdims=False)]
  transfers between devices with their start and end apart: 10 -> 0, of which waited for: 10 -> 0; matrix products, arithmetic and copies ran while one was open for 1% -> 0% of each run, Pallas kernels for 0% -> 0%
where the time goes in v1:
time: 50.5 us; the launch traced here: 50.3 us
  Pallas kernels  48.9 us (97%)
  local copies, waits for them, and re-layouts  1.44 us (3%)
    pallas_call x1, Pallas kernels, shards(): pl.pallas_call(functools.partial(kernel, p, experts), out_shape=jax.Shape...  48.9 us
    unnamed x1, local copies, waits for them, and re-layouts  1.44 us

profile of v1, /device:TPU:0, one launch (start us, length us, event | category | flops | bytes accessed | tf_op | source)
XLA Modules:
  0.0 50.3 jit_solution(18034269126900073962)
XLA Ops:
  0.0 48.9 %moe_decode.1 = bf16[4,6144]{1,0:T(4,128)(2,1)} custom-call(bf16[4,6144]{1,0:T(4,128)(2,1)} %tok_ref.1, s32[2,4]{1,0:T(2,128)} %bitcast.3, bf16[4,6144]{1,0:T(4,128)(2,1)} %bitcast.2, bf16[1,6144,2048]{2,1,0:T(8,128)(2,1)} %gate_ref.1, bf16[1,6144,2048]{2,1,0:T(8,128)(2,1)} %up_ref.1, bf16[1,2048,6144]{2,1,0:T(8,128)(2,1)} %down_ref.1), custom_call_target="tpu_custom_call" | custom-call | flops 4831838208 | bytes 75497472 | tf_op jit(solution)/shard_map/moe_decode/pallas_call | solution.py:301
  48.9 1.4 %copy.8 = bf16[4,6144]{1,0:T(4,128)(2,1)} copy(bf16[4,6144]{1,0:T(4,128)(2,1)} %moe_decode.1) | data formatting | bytes 98304

commit v2 on v1

--- a/solution.py
+++ b/solution.py
@@ -12,6 +12,8 @@
 BF16 = jnp.bfloat16
 LANES = 128
 PLANE = 4
+SPLIT = 32
+LAG = 2
 ROWS = 16
 
 
@@ -26,6 +28,8 @@
         self.pieces = ROWS // tok
         self.piece = width // self.pieces
         self.ext = self.piece + LANES
+        middle = self.ext // LANES // 2 * LANES
+        self.spans = ((0, middle), (middle, self.ext - middle))
         self.tokens = devices * tok
         self.half = self.tokens // 2
         self.quarter = self.tokens // 4
@@ -91,14 +95,30 @@
 
     lane = lax.broadcasted_iota(jnp.int32, (p.tok, LANES), 1)
     line = lax.broadcasted_iota(jnp.int32, (p.tok, LANES), 0)
-    ids = jnp.zeros((p.tok, LANES), jnp.int32)
+    id_a = jnp.zeros((p.tok, LANES), jnp.int32)
+    id_b = id_a
     for t in range(p.tok):
-        named = jnp.where(lane < LANES // 2, ids_ref[0, t], ids_ref[1, t])
-        ids = jnp.where(line == t, named, ids)
+        id_a = jnp.where(line == t, ids_ref[0, t], id_a)
+        id_b = jnp.where(line == t, ids_ref[1, t], id_b)
+    own = tok_ref[...].astype(F32)
+    logit_a = jnp.zeros((p.tok, LANES), F32)
+    logit_b = logit_a
+    for expert in range(experts):
+        row = router_ref[pl.ds(expert, 1), :].astype(F32)
+        logit = jnp.sum(own * row, axis=1, keepdims=True)
+        logit_a = jnp.where(id_a == expert, logit, logit_a)
+        logit_b = jnp.where(id_b == expert, logit, logit_b)
+    named = lane % SPLIT
+    weight = jnp.where(named == id_a, 1.0 / (1.0 + jnp.exp(logit_b - logit_a)), 0.0)
+    weight += jnp.where(named == id_b, 1.0 / (1.0 + jnp.exp(logit_a - logit_b)), 0.0)
+    high = weight.astype(BF16).astype(F32)
+    middle = (weight - high).astype(BF16).astype(F32)
+    terms = jnp.where(lane < SPLIT, high, jnp.where(lane < 2 * SPLIT, middle, weight - high - middle))
+    terms = jnp.where(lane < 3 * SPLIT, terms, 0.0)
     for c in range(p.pieces):
         rows = pl.ds(c * p.tok, p.tok)
         stage[rows, pl.ds(0, p.piece)] = tok_ref[:, pl.ds(c * p.piece, p.piece)].astype(F32)
-        stage[rows, pl.ds(p.piece, LANES)] = ids.astype(F32)
+        stage[rows, pl.ds(p.piece, LANES)] = terms
     x[me] = stage[...].astype(BF16)
 
     pl.semaphore_wait(barrier, p.slots + 1)
@@ -109,10 +129,21 @@
         copy.start()
         started.append(copy)
 
-    for d in range(1, p.slots):
-        send(remote(x.at[me], x.at[me], gs_z.at[d], gr_z.at[d], z_peers[d - 1]))
-    send(remote(x.at[me], x.at[me], gs_y.at[0], gr_y.at[0], y_peer))
-    send(remote(x.at[me], x.at[me], gs_c.at[0], gr_c.at[0], core_peer))
+    def block_copy(block, h, send_sems, recv_sems, at, device):
+        cols = pl.ds(*p.spans[h])
+        ref = x.at[block, :, cols]
+        return remote(ref, ref, send_sems.at[h, at], recv_sems.at[h, at], device)
+
+    def z_block(d):
+        return lax.rem(slot + p.slots - d, p.slots) * PLANE
+
+    spans = range(len(p.spans))
+    for h in spans:
+        for d in range(1, p.slots):
+            send(block_copy(me, h, gs_z, gr_z, d, z_peers[d - 1]))
+        send(block_copy(me, h, gs_y, gr_y, 0, y_peer))
+    for h in spans:
+        send(block_copy(me, h, gs_c, gr_c, 0, core_peer))
 
     for n in range(1, p.n_steps):
         for m in range(p.per_n):
@@ -120,39 +151,42 @@
     for j in range(p.first, p.downs):
         down_copy(j).start()
 
-    for d in range(1, p.slots):
-        block = lax.rem(slot + p.slots - d, p.slots) * PLANE + e
-        remote(x.at[block], x.at[block], gs_z.at[d], gr_z.at[d], me ^ 1).wait_recv()
-        send(remote(x.at[block], x.at[block], gs_y.at[d], gr_y.at[d], y_peer))
-        send(remote(x.at[block], x.at[block], gs_c.at[d], gr_c.at[d], core_peer))
-    for d in range(p.slots):
-        block = lax.rem(slot + p.slots - d, p.slots) * PLANE + (1 - ypos) * 2 + core
-        remote(x.at[block], x.at[block], gs_y.at[d], gr_y.at[d], y_peer).wait_recv()
-        at = p.slots + d
-        send(remote(x.at[block], x.at[block], gs_c.at[at], gr_c.at[at], core_peer))
-    for d in range(p.slots):
+    for h in spans:
+        for d in range(1, p.slots):
+            block = z_block(d) + e
+            block_copy(block, h, gs_z, gr_z, d, core_peer).wait_recv()
+            send(block_copy(block, h, gs_y, gr_y, d, y_peer))
+            send(block_copy(block, h, gs_c, gr_c, d, core_peer))
+    for h in spans:
+        for d in range(p.slots):
+            block = z_block(d) + (1 - ypos) * 2 + core
+            block_copy(block, h, gs_y, gr_y, d, y_peer).wait_recv()
+            send(block_copy(block, h, gs_c, gr_c, p.slots + d, core_peer))
+    for h in spans:
         for side in range(2):
             ye = ypos if side == 0 else 1 - ypos
-            block = lax.rem(slot + p.slots - d, p.slots) * PLANE + ye * 2 + (1 - core)
-            at = side * p.slots + d
-            remote(x.at[block], x.at[block], gs_c.at[at], gr_c.at[at], core_peer).wait_recv()
-
-    blocks = p.quarter
-    row_in = lax.broadcasted_iota(jnp.int32, (p.quarter, p.devices * ROWS), 0)
-    col_in = lax.broadcasted_iota(jnp.int32, (p.quarter, p.devices * ROWS), 1)
-    for q in range(PLANE):
-        dest_core, dest_y = q // 2, q % 2
-        device = (row_in // p.tok) * PLANE + dest_y * 2 + dest_core
-        for c in range(p.pieces):
-            pick = (col_in == device * ROWS + c * p.tok + row_in % p.tok)
-            pick = jnp.where(pick, 1.0, 0.0).astype(BF16)
-            flat = x[...].reshape(p.devices * ROWS, p.ext)
-            got = jnp.dot(pick, flat, preferred_element_type=F32)
-            lhs[pl.ds(q * p.quarter, p.quarter), pl.ds(c * p.piece, p.piece)] = (
-                got[:, : p.piece].astype(BF16)
-            )
-            if c == 0:
-                table[pl.ds(q * p.quarter, p.quarter), :] = got[:, p.piece:]
+            for d in range(p.slots):
+                block = z_block(d) + ye * 2 + (1 - core)
+                at = side * p.slots + d
+                block_copy(block, h, gs_c, gr_c, at, core_peer).wait_recv()
+
+    row_in = lax.broadcasted_iota(jnp.int32, (p.tokens, p.devices * ROWS), 0)
+    col_in = lax.broadcasted_iota(jnp.int32, (p.tokens, p.devices * ROWS), 1)
+    dest = row_in // p.quarter
+    device = (row_in % p.quarter) // p.tok * PLANE + dest % 2 * 2 + dest // 2
+    col_in = col_in - (device * ROWS + row_in % p.tok)
+    flat = x[...].reshape(p.devices * ROWS, p.ext)
+    for c in range(p.pieces):
+        pick = jnp.where(col_in == c * p.tok, 1.0, 0.0).astype(BF16)
+        got = jnp.dot(
+            pick, flat if c == 0 else flat[:, : p.piece], preferred_element_type=F32
+        )
+        lhs[:, pl.ds(c * p.piece, p.piece)] = got[:, : p.piece].astype(BF16)
+        if c == 0:
+            lane = lax.broadcasted_iota(jnp.int32, (p.tokens, LANES), 1)
+            terms = jnp.where(lane % SPLIT == e, got[:, p.piece :], 0.0)
+            weight = jnp.sum(terms, axis=1, keepdims=True)
+            table[...] = jnp.broadcast_to(weight, table.shape)
 
     @pl.loop(0, p.n_steps)
     def _(n):
@@ -174,19 +208,6 @@
             def _():
                 down_copy(n * p.per_n + m).start()
 
-    logits = lax.dot_general(
-        lhs[...], router_ref[...], (((1,), (1,)), ((), ())), preferred_element_type=F32
-    )
-    ids = table[...]
-    id_a, id_b = ids[:, 0:1], ids[:, LANES // 2 : LANES // 2 + 1]
-    iota = lax.broadcasted_iota(jnp.int32, logits.shape, 1).astype(F32)
-    logit_a = jnp.sum(jnp.where(iota == id_a, logits, 0.0), axis=1, keepdims=True)
-    logit_b = jnp.sum(jnp.where(iota == id_b, logits, 0.0), axis=1, keepdims=True)
-    mine = e.astype(F32)
-    weight = jnp.where(id_a == mine, 1.0 / (1.0 + jnp.exp(logit_b - logit_a)), 0.0)
-    weight += jnp.where(id_b == mine, 1.0 / (1.0 + jnp.exp(logit_a - logit_b)), 0.0)
-    table[...] = jnp.broadcast_to(weight, table.shape)
-
     def copy_a(g):
         return remote(a_send.at[g], a_recv.at[g], sa.at[g], ra.at[g], core_peer)
 
@@ -237,19 +258,19 @@
         for d in range(1, p.slots):
             copy_c(g, d).start()
 
-    @pl.loop(0, p.groups + 2)
+    @pl.loop(0, p.groups + 2 * LAG)
     def _(it):
         @pl.when(it < p.groups)
         def _():
             compute(it)
 
-        @pl.when((it >= 1) & (it < p.groups + 1))
+        @pl.when((it >= LAG) & (it < p.groups + LAG))
         def _():
-            second(it - 1)
-
-        @pl.when(it >= 2)
+            second(it - LAG)
+
+        @pl.when(it >= 2 * LAG)
         def _():
-            third(it - 2)
+            third(it - 2 * LAG)
 
     @pl.loop(0, p.groups)
     def _(g):
@@ -293,8 +314,8 @@
         pltpu.VMEM((p.groups, p.slots, ROWS, p.part), BF16),
         pltpu.VMEM((ROWS, p.part), F32),
         dma((p.buffers,)),
-        dma((p.slots,)), dma((p.slots,)), dma((p.slots,)), dma((p.slots,)),
-        dma((2 * p.slots,)), dma((2 * p.slots,)),
+        dma((2, p.slots)), dma((2, p.slots)), dma((2, p.slots)), dma((2, p.slots)),
+        dma((2, 2 * p.slots)), dma((2, 2 * p.slots)),
         dma((p.groups,)), dma((p.groups,)), dma((p.groups,)), dma((p.groups,)),
         dma((p.groups, p.slots)), dma((p.groups, p.slots)),
     ]

time: 50.5 us -> 45.6 us (0.903)
  Pallas kernels: 48.9 us -> 43.9 us
    pallas_call x1, Pallas kernels: 48.9 us -> 43.9 us  [shards(): pl.pallas_call(functools.partial(kernel, p, experts), out_shape=jax.Shape...]
where the time goes in v2:
time: 45.6 us; the launch traced here: 45.4 us
  Pallas kernels  43.9 us (96%)
  local copies, waits for them, and re-layouts  1.44 us (3%)
    pallas_call x1, Pallas kernels, shards(): pl.pallas_call(functools.partial(kernel, p, experts), out_shape=jax.Shape...  43.9 us
    unnamed x1, local copies, waits for them, and re-layouts  1.44 us

profile of v2, /device:TPU:0, one launch (start us, length us, event | category | flops | bytes accessed | tf_op | source)
XLA Modules:
  0.0 45.4 jit_solution(8100088430296919173)
XLA Ops:
  0.0 43.9 %moe_decode.1 = bf16[4,6144]{1,0:T(4,128)(2,1)} custom-call(bf16[4,6144]{1,0:T(4,128)(2,1)} %tok_ref.1, s32[2,4]{1,0:T(2,128)} %bitcast.3, bf16[4,6144]{1,0:T(4,128)(2,1)} %bitcast.2, bf16[1,6144,2048]{2,1,0:T(8,128)(2,1)} %gate_ref.1, bf16[1,6144,2048]{2,1,0:T(8,128)(2,1)} %up_ref.1, bf16[1,2048,6144]{2,1,0:T(8,128)(2,1)} %down_ref.1), custom_call_target="tpu_custom_call" | custom-call | flops 4831838208 | bytes 75497472 | tf_op jit(solution)/shard_map/moe_decode/pallas_call | solution.py:322
  44.0 1.4 %copy.8 = bf16[4,6144]{1,0:T(4,128)(2,1)} copy(bf16[4,6144]{1,0:T(4,128)(2,1)} %moe_decode.1) | data formatting | bytes 98304

commit v3 on v2

--- a/solution.py
+++ b/solution.py
@@ -13,7 +13,7 @@
 LANES = 128
 PLANE = 4
 SPLIT = 32
-LAG = 2
+LAG = 1
 ROWS = 16
 
 
@@ -42,7 +42,7 @@
         self.down_cols = divisor_at_most(width, 512)
         self.downs = width // self.down_cols
         self.buffers = max(self.first, self.downs)
-        self.group = 2
+        self.group = 3
         self.groups = self.downs // self.group
         self.cols = self.group * self.down_cols
         self.part = self.cols // self.pieces

time: 45.6 us -> 47.1 us (1.033)
  Pallas kernels: 43.9 us -> 45.4 us
    pallas_call x1, Pallas kernels: 43.9 us -> 45.4 us  [shards(): pl.pallas_call(functools.partial(kernel, p, experts), out_shape=jax.Shape...]
where the time goes in v3:
time: 47.1 us; the launch traced here: 46.8 us
  Pallas kernels  45.4 us (96%)
  local copies, waits for them, and re-layouts  1.44 us (3%)
    pallas_call x1, Pallas kernels, shards(): pl.pallas_call(functools.partial(kernel, p, experts), out_shape=jax.Shape...  45.4 us
    unnamed x1, local copies, waits for them, and re-layouts  1.44 us

profile of v3, /device:TPU:0, one launch (start us, length us, event | category | flops | bytes accessed | tf_op | source)
XLA Modules:
  0.0 46.8 jit_solution(14396306671459962227)
XLA Ops:
  0.0 45.4 %moe_decode.1 = bf16[4,6144]{1,0:T(4,128)(2,1)} custom-call(bf16[4,6144]{1,0:T(4,128)(2,1)} %tok_ref.1, s32[2,4]{1,0:T(2,128)} %bitcast.3, bf16[4,6144]{1,0:T(4,128)(2,1)} %bitcast.2, bf16[1,6144,2048]{2,1,0:T(8,128)(2,1)} %gate_ref.1, bf16[1,6144,2048]{2,1,0:T(8,128)(2,1)} %up_ref.1, bf16[1,2048,6144]{2,1,0:T(8,128)(2,1)} %down_ref.1), custom_call_target="tpu_custom_call" | custom-call | flops 4831838208 | bytes 75497472 | tf_op jit(solution)/shard_map/moe_decode/pallas_call | solution.py:322
  45.4 1.4 %copy.8 = bf16[4,6144]{1,0:T(4,128)(2,1)} copy(bf16[4,6144]{1,0:T(4,128)(2,1)} %moe_decode.1) | data formatting | bytes 98304
